TPU v7x, 256 devices: a whole 4x4x8 slice. The times are simulated.
256 devices in a mesh: outer: 32 (over y_lo, z, core), inner: 8 (over y_hi, x).
Axes of the slice: x: 4, y: 4 (y_hi: 2, y_lo: 2; y = y_hi * 2 + y_lo), z: 8, core: 2. Of those that a mesh axis runs over, the one named last changes fastest.
Arguments:
- queries: bfloat16 [65536, 1024], P(('outer', 'inner')), may hold values from -1.6953125 to 1.6953125
- key_rows: bfloat16 [65536, 128], P(('outer', 'inner')), may hold values from -1.6953125 to 1.6953125
- value_rows: bfloat16 [65536, 128], P(('outer', 'inner')), may hold values from -6 to 6
- outputs: bfloat16 [65536, 1024], P(('outer', 'inner')), may hold values from -4 to 4
- out_grad: bfloat16 [65536, 1024], P(('outer', 'inner')), may hold values from -32 to 32
- log_norm: float32 [8, 65536], P(None, ('outer', 'inner')), may hold values from 6.5 to 8
- shard_pos: int32 [512], replicated, may hold values from 0 to 511, each once
Outputs:
- query_grad: bfloat16 [65536, 1024], P(('outer', 'inner'))
- key_grad: bfloat16 [65536, 128], P(('outer', 'inner'))
- value_grad: bfloat16 [65536, 128], P(('outer', 'inner'))
Inputs may be any that keep to these rules, and one draw needn't show every extreme that they name: `shard_pos`: each of 0 to 511 appears once.
All inputs are finite; a program needn't handle non-finite values.
Results may differ from a plain program's by a relative error of at most 0.0049.
Values may be sent and summed in bfloat16 or wider, within the bound.
A program may use at most 128 MiB of HBM per device.

v0:
```python
import functools

import jax
import jax.numpy as jnp
from jax import lax
from jax.experimental import pallas as pl
from jax.experimental.pallas import tpu as pltpu
from jax.sharding import PartitionSpec as P

F32 = jnp.float32
BF16 = jnp.bfloat16
MESH = pl.DeviceIdType.MESH
LOG2E = 1.4426950408889634
HIDDEN = 1e30

FAR = -1
STEPS = (
    (0, 0, 0),
    (1, 0, 0),
    (1, 0, 1),
    (0, 1, 0),
    (1, 1, 0),
    (1, 1, 1),
    (2, 0, 0),
    (2, 0, 1),
    (2, 1, 0),
    (2, 1, 1),
    (FAR, 1, 1),
    (FAR, 0, 1),
)


def dot(a, b):
    return jnp.dot(a, b, preferred_element_type=F32)


def dot_nt(a, b):
    return lax.dot_general(a, b, (((1,), (1,)), ((), ())), preferred_element_type=F32)


def at_step(t, values):
    return sum(jnp.where(t == n, value, 0) for n, value in enumerate(values))


def kernel(
    sizes,
    q_hbm, k_hbm, v_hbm, o_hbm, g_hbm, norm_hbm, pos_ref,
    dq_out, dk_out, dv_out,
    qs, gs, os, qt, gt, kv, norm, cols, cols_in, lse, delta, hidden,
    dq, dkv, staged, from_x, from_z, dq_send, dq_recv, dq_final, dkv_final,
    load_q, load_g, load_o, load_kv, load_norm, store_dq, store_dkv,
    swap_send, swap_recv, fwd_send, fwd_recv, ret_send, x_recv, z_recv,
):
    n_outer, n_inner, heads, rows, hd = sizes
    shard = rows // 2
    scale = hd**-0.5
    outer, inner = lax.axis_index("outer"), lax.axis_index("inner")
    core = lax.rem(outer, 2)

    def chip(dc, e=0):
        return (
            lax.rem(outer + 2 * dc + n_outer, n_outer),
            lax.rem(inner + e + n_inner, n_inner),
        )

    sibling = (outer + 1 - 2 * core, inner)

    def remote(src, dst, send, recv, to):
        return pltpu.make_async_remote_copy(
            src_ref=src, dst_ref=dst, send_sem=send, recv_sem=recv,
            device_id=to, device_id_type=MESH,
        )

    def loads(src, dst, sem):
        return [
            pltpu.make_async_copy(
                src.at[:, pl.ds(h * hd, hd)], dst.at[pl.ds(h * rows, rows)], sem.at[h]
            )
            for h in range(heads)
        ]

    kv_loads = [
        pltpu.make_async_copy(ref, kv.at[0, n], load_kv.at[n])
        for n, ref in enumerate((k_hbm, v_hbm))
    ]
    norm_load = pltpu.make_async_copy(norm_hbm, norm, load_norm)
    q_loads = loads(q_hbm, qs.at[0], load_q)
    g_loads = loads(g_hbm, gs.at[0], load_g)
    o_loads = loads(o_hbm, os, load_o)

    swap_q = remote(qs.at[0], qs.at[1], swap_send.at[0], swap_recv.at[0], sibling)
    swap_g = remote(gs.at[0], gs.at[1], swap_send.at[1], swap_recv.at[1], sibling)
    swap_cols = remote(cols, cols_in, swap_send.at[2], swap_recv.at[2], sibling)
    swap_dq = remote(dq_send, dq_recv, swap_send.at[3], swap_recv.at[3], sibling)

    def to_z(dc):
        return remote(
            kv.at[2 * dc], kv.at[2 * dc + 2], fwd_send.at[2 * dc], fwd_recv.at[2 * dc + 2], chip(1)
        )

    def to_x(dc):
        return remote(
            kv.at[2 * dc], kv.at[2 * dc + 1], fwd_send.at[2 * dc + 1], fwd_recv.at[2 * dc + 1],
            chip(0, 1),
        )

    def back_x(dc):
        slot = 2 * dc + 1
        return remote(
            staged.at[slot], from_x.at[dc], ret_send.at[slot], x_recv.at[dc], chip(0, -1)
        )

    def back_z(dc):
        slot = 2 * dc
        return remote(
            staged.at[slot], from_z.at[dc], ret_send.at[slot], z_recv.at[dc], chip(-dc)
        )

    for copy in (*kv_loads, *q_loads, *g_loads, norm_load, *o_loads):
        copy.start()
    partners = [sibling, chip(0, 1), chip(0, -1)]
    for dc in (1, 2, 3):
        partners += [chip(dc), chip(-dc)]
    barrier = pltpu.get_barrier_semaphore()
    for partner in partners:
        pl.semaphore_signal(barrier, inc=1, device_id=partner, device_id_type=MESH)

    dkv[...] = jnp.zeros_like(dkv)
    dq[...] = jnp.zeros_like(dq)
    for copy in kv_loads:
        copy.wait()
    pl.semaphore_wait(barrier, len(partners))
    to_z(0).start()
    to_x(0).start()
    for copy in q_loads:
        copy.wait()
    swap_q.start()
    for copy in g_loads:
        copy.wait()
    swap_g.start()

    norm_load.wait()
    lane = lax.broadcasted_iota(jnp.int32, (rows, hd), 1)
    padded = jnp.concatenate([norm[...] * LOG2E, jnp.zeros((hd - heads, rows), F32)], 0)
    cols[0] = padded.T
    for copy in o_loads:
        copy.wait()
    packed = jnp.zeros((rows, hd), F32)
    for h in range(heads):
        part = pl.ds(h * rows, rows)
        product = gs[0, part, :].astype(F32) * os[part, :].astype(F32)
        packed = jnp.where(lane == h, jnp.sum(product, axis=1, keepdims=True), packed)
    cols[1] = packed
    swap_cols.start()

    def prepare(side, source):
        for h in range(heads):
            part = pl.ds(h * rows, rows)
            lse[side, part, :] = jnp.broadcast_to(source[0, :, h : h + 1], (rows, hd))
            delta[side, part, :] = jnp.broadcast_to(source[1, :, h : h + 1], (rows, hd))
            qt[side, :, part] = qs[side, part, :].T
            gt[side, :, part] = gs[side, part, :].T

    prepare(0, cols)

    def positions(outer_index, inner_index, dim):
        first = 2 * (outer_index * n_inner + inner_index)
        at = lax.broadcasted_iota(jnp.int32, (rows, rows), dim)
        start = jnp.where(at < shard, pos_ref[first], pos_ref[first + 1] - 1)
        return start * shard + at

    chunk = heads * rows // 2

    def step(side, dc, e):
        slot = 2 * dc + e
        q_pos = positions(outer + side * (1 - 2 * core), inner, 0)
        kv_outer, kv_inner = chip(-dc, -e)
        k_pos = positions(kv_outer, kv_inner, 1)
        hidden[...] = jnp.where(k_pos <= q_pos, 0.0, HIDDEN)
        k, v = kv[slot, 0], kv[slot, 1]

        def front(j):
            part = pl.ds(j * chunk, chunk)
            return dot_nt(qs[side, part, :], k), dot_nt(gs[side, part, :], v)

        def middle(j, s, dp):
            part = pl.ds(j * chunk, chunk)
            row_lse = jnp.tile(lse[side, part, :], (1, rows // hd))
            row_delta = jnp.tile(delta[side, part, :], (1, rows // hd))
            exponent = s * (scale * LOG2E) - row_lse
            exponent = exponent.reshape(-1, rows, rows) - hidden[...][None]
            weights = jnp.exp2(exponent.reshape(chunk, rows))
            score_grad = weights * (dp - row_delta) * scale
            return weights.astype(BF16), score_grad.astype(BF16)

        def back(j, weights, score_grad):
            part = pl.ds(j * chunk, chunk)
            dq[side, part, :] += dot(score_grad, k)
            return dot(qt[side, :, part], score_grad), dot(gt[side, :, part], weights)

        ahead = front(0)
        dk = dv = None
        for j in range(2):
            now, ahead = ahead, front(1) if j == 0 else None
            dk_part, dv_part = back(j, *middle(j, *now))
            dk, dv = (dk_part, dv_part) if j == 0 else (dk + dk_part, dv + dv_part)
        dkv[slot, 0] += dk
        dkv[slot, 1] += dv

    far = 3 * core

    def on_far(body):
        pl.when(core == 1)(body)

    def send_x(dc):
        staged[2 * dc + 1] = dkv[2 * dc + 1].astype(BF16)
        back_x(dc).start()

    def send_z(dc):
        back_x(dc).wait_recv()
        staged[2 * dc] = (dkv[2 * dc] + from_x[dc].astype(F32)).astype(BF16)
        back_z(dc).start()

    def before(t):
        @pl.when(t == 1)
        def _():
            to_z(0).wait_recv()
            to_z(1).start()
            to_x(1).start()
            swap_q.wait_recv()
            swap_g.wait_recv()
            swap_cols.wait_recv()
            prepare(1, cols_in)

        @pl.when(t == 3)
        def _():
            to_x(0).wait_recv()

        @pl.when(t == 4)
        def _():
            to_z(1).wait_recv()
            on_far(lambda: to_z(2).start())
            to_x(2).start()
            to_x(1).wait_recv()

        @pl.when((t == 7) & (core == 1))
        def _():
            to_z(2).wait_recv()
            to_x(3).start()

        @pl.when(t == 8)
        def _():
            to_x(2).wait_recv()

        @pl.when((t == 10) & (core == 1))
        def _():
            to_x(3).wait_recv()

    def after(t):
        @pl.when(t == 5)
        def _():
            send_x(1)

        @pl.when(t == 7)
        def _():
            send_z(1)

        @pl.when(t == 9)
        def _():
            send_x(2)

        @pl.when(t == 10)
        def _():
            send_x(0)
            on_far(lambda: send_x(3))

    def body(t, carry):
        before(t)
        dc = at_step(t, [far if dc == FAR else dc for dc, _, _ in STEPS])
        e = at_step(t, [e for _, e, _ in STEPS])
        side = at_step(t, [side for _, _, side in STEPS])
        step(side, dc, e)
        after(t)
        return carry

    lax.fori_loop(0, len(STEPS), body, 0)

    dq_send[...] = dq[1].astype(BF16)
    swap_dq.start()
    send_z(2)
    on_far(lambda: send_z(3))

    swap_dq.wait_recv()
    stores = []
    for h in range(heads):
        part = pl.ds(h * rows, rows)
        dq_final[part, :] = (dq[0, part, :] + dq_recv[part, :].astype(F32)).astype(BF16)
        copy = pltpu.make_async_copy(
            dq_final.at[part], dq_out.at[:, pl.ds(h * hd, hd)], store_dq.at[h]
        )
        copy.start()
        stores.append(copy)

    back_x(0).wait_recv()
    back_z(1).wait_recv()
    dkv[0] += from_x[0].astype(F32) + from_z[1].astype(F32)
    back_z(2).wait_recv()
    dkv[0] += from_z[2].astype(F32)

    @pl.when(core == 1)
    def _():
        back_z(3).wait_recv()
        dkv[0] += from_z[3].astype(F32)

    dkv_final[0] = dkv[0, 0].T.astype(BF16)
    dkv_final[1] = dkv[0, 1].T.astype(BF16)
    for n, ref in enumerate((dk_out, dv_out)):
        copy = pltpu.make_async_copy(dkv_final.at[n], ref, store_dkv.at[n])
        copy.start()
        stores.append(copy)

    for copy in (swap_q, swap_g, swap_cols, swap_dq):
        copy.wait_send()
    for copy in (to_z(0), to_z(1), to_x(0), to_x(1), to_x(2)):
        copy.wait_send()
    for copy in (back_x(0), back_x(1), back_x(2), back_z(1), back_z(2)):
        copy.wait_send()

    @pl.when(core == 1)
    def _():
        for copy in (to_z(2), to_x(3), back_x(3), back_z(3)):
            copy.wait_send()

    for copy in stores:
        copy.wait()


def local(mesh, queries, key_rows, value_rows, outputs, out_grad, log_norm, shard_pos):
    rows, hd = key_rows.shape
    heads = queries.shape[1] // hd
    flat = heads * rows
    sizes = (mesh.shape["outer"], mesh.shape["inner"], heads, rows, hd)
    dma = pltpu.SemaphoreType.DMA
    scratch = [
        pltpu.VMEM((2, flat, hd), BF16),
        pltpu.VMEM((2, flat, hd), BF16),
        pltpu.VMEM((flat, hd), BF16),
        pltpu.VMEM((2, hd, flat), BF16),
        pltpu.VMEM((2, hd, flat), BF16),
        pltpu.VMEM((8, 2, rows, hd), BF16),
        pltpu.VMEM((heads, rows), F32),
        pltpu.VMEM((2, rows, hd), F32),
        pltpu.VMEM((2, rows, hd), F32),
        pltpu.VMEM((2, flat, hd), F32),
        pltpu.VMEM((2, flat, hd), F32),
        pltpu.VMEM((rows, rows), F32),
        pltpu.VMEM((2, flat, hd), F32),
        pltpu.VMEM((8, 2, hd, rows), F32),
        pltpu.VMEM((8, 2, hd, rows), BF16),
        pltpu.VMEM((4, 2, hd, rows), BF16),
        pltpu.VMEM((4, 2, hd, rows), BF16),
        pltpu.VMEM((flat, hd), BF16),
        pltpu.VMEM((flat, hd), BF16),
        pltpu.VMEM((flat, hd), BF16),
        pltpu.VMEM((2, rows, hd), BF16),
        dma((heads,)),
        dma((heads,)),
        dma((heads,)),
        dma((2,)),
        dma,
        dma((heads,)),
        dma((2,)),
        dma((4,)),
        dma((4,)),
        dma((8,)),
        dma((8,)),
        dma((8,)),
        dma((4,)),
        dma((4,)),
    ]
    hbm = pl.BlockSpec(memory_space=pl.ANY)
    return pl.pallas_call(
        functools.partial(kernel, sizes),
        out_shape=(
            jax.ShapeDtypeStruct(queries.shape, BF16),
            jax.ShapeDtypeStruct(key_rows.shape, BF16),
            jax.ShapeDtypeStruct(value_rows.shape, BF16),
        ),
        in_specs=[hbm] * 6 + [pl.BlockSpec(memory_space=pltpu.SMEM)],
        out_specs=(hbm,) * 3,
        scratch_shapes=scratch,
        compiler_params=pltpu.CompilerParams(
            collective_id=0, has_side_effects=True, vmem_limit_bytes=48 * 2**20
        ),
        name="window_grads",
    )(queries, key_rows, value_rows, outputs, out_grad, log_norm, shard_pos)


def solution(mesh):
    rows = P(("outer", "inner"), None)
    return jax.shard_map(
        functools.partial(local, mesh),
        mesh=mesh,
        in_specs=(rows, rows, rows, rows, rows, P(None, ("outer", "inner")), P()),
        out_specs=(rows, rows, rows),
        check_vma=False,
    )
```

profile of v0, /device:TPU:7, one launch (start us, length us, event | category | flops | bytes accessed | tf_op | source)
XLA Modules:
  0.0 55.1 jit_solution(14854718809736122098)
XLA Ops:
  0.6 0.0 copy-start
  0.6 1.0 %copy-done = bf16[256,1024]{1,0:T(8,128)(2,1)S(1)} copy-done((bf16[256,1024]{1,0:T(8,128)(2,1)S(1)}, bf16[256,1024]{1,0:T(8,128)(2,1)}, u32[]{:S(2)}) %copy-start) | copy-done | bytes 524312
  1.7 0.0 copy-start.1
  1.7 1.0 %copy-done.1 = bf16[256,1024]{1,0:T(8,128)(2,1)S(1)} copy-done((bf16[256,1024]{1,0:T(8,128)(2,1)S(1)}, bf16[256,1024]{1,0:T(8,128)(2,1)}, u32[]{:S(2)}) %copy-start.1) | copy-done | bytes 524312
  2.7 0.0 copy-start.2
  2.7 1.0 %copy-done.2 = bf16[256,1024]{1,0:T(8,128)(2,1)S(1)} copy-done((bf16[256,1024]{1,0:T(8,128)(2,1)S(1)}, bf16[256,1024]{1,0:T(8,128)(2,1)}, u32[]{:S(2)}) %copy-start.2) | copy-done | bytes 524312
  3.8 0.0 copy-start.3
  3.8 0.8 %copy-done.3 = bf16[256,128]{1,0:T(8,128)(2,1)S(1)} copy-done((bf16[256,128]{1,0:T(8,128)(2,1)S(1)}, bf16[256,128]{1,0:T(8,128)(2,1)}, u32[]{:S(2)}) %copy-start.3) | copy-done | bytes 65560
  4.6 0.0 copy-start.4
  4.6 0.8 %copy-done.4 = bf16[256,128]{1,0:T(8,128)(2,1)S(1)} copy-done((bf16[256,128]{1,0:T(8,128)(2,1)S(1)}, bf16[256,128]{1,0:T(8,128)(2,1)}, u32[]{:S(2)}) %copy-start.4) | copy-done | bytes 65560
  5.4 0.0 copy-start.5
  5.4 0.7 %copy-done.5 = f32[8,256]{1,0:T(8,128)S(1)} copy-done((f32[8,256]{1,0:T(8,128)S(1)}, f32[8,256]{1,0:T(8,128)}, u32[]{:S(2)}) %copy-start.5) | copy-done | bytes 8216
  6.1 0.0 copy-start.6
  6.1 0.7 %copy-done.6 = s32[512]{0:T(512)S(1)} copy-done((s32[512]{0:T(512)S(1)}, s32[512]{0:T(512)}, u32[]{:S(2)}) %copy-start.6) | copy-done | bytes 2072
  6.8 46.3 %window_grads.1 = (bf16[256,1024]{1,0:T(8,128)(2,1)S(1)}, bf16[256,128]{1,0:T(8,128)(2,1)S(1)}, bf16[256,128]{1,0:T(8,128)(2,1)S(1)}) custom-call(bf16[256,1024]{1,0:T(8,128)(2,1)S(1)} %copy-done, bf16[256,128]{1,0:T(8,128)(2,1)S(1)} %copy-done.3, bf16[256,128]{1,0:T(8,128)(2,1)S(1)} %copy-done.4, bf16[256,1024]{1,0:T(8,128)(2,1)S(1)} %copy-done.1, ...), custom_call_target="tpu_custom_call" | custom-call | tf_op jit(solution)/shard_map/window_grads/pallas_call | solution.py:382
  53.1 0.8 %copy.13 = bf16[256,1024]{1,0:T(8,128)(2,1)} copy(bf16[256,1024]{1,0:T(8,128)(2,1)S(1)} %get-tuple-element.6) | data formatting | bytes 1048576
  53.9 0.6 %copy.14 = bf16[256,128]{1,0:T(8,128)(2,1)} copy(bf16[256,128]{1,0:T(8,128)(2,1)S(1)} %get-tuple-element.7) | data formatting | bytes 131072
  54.5 0.6 %copy.15 = bf16[256,128]{1,0:T(8,128)(2,1)} copy(bf16[256,128]{1,0:T(8,128)(2,1)S(1)} %get-tuple-element.8) | data formatting | bytes 131072
Async XLA Ops:
  0.6 1.0 %copy-start = (bf16[256,1024]{1,0:T(8,128)(2,1)S(1)}, bf16[256,1024]{1,0:T(8,128)(2,1)}, u32[]{:S(2)}) copy-start(bf16[256,1024]{1,0:T(8,128)(2,1)} %q_hbm.1) | copy-start | bytes 1572868
  1.7 1.0 %copy-start.1 = (bf16[256,1024]{1,0:T(8,128)(2,1)S(1)}, bf16[256,1024]{1,0:T(8,128)(2,1)}, u32[]{:S(2)}) copy-start(bf16[256,1024]{1,0:T(8,128)(2,1)} %o_hbm.1) | copy-start | bytes 1572868
  2.7 1.0 %copy-start.2 = (bf16[256,1024]{1,0:T(8,128)(2,1)S(1)}, bf16[256,1024]{1,0:T(8,128)(2,1)}, u32[]{:S(2)}) copy-start(bf16[256,1024]{1,0:T(8,128)(2,1)} %g_hbm.1) | copy-start | bytes 1572868
  3.8 0.8 %copy-start.3 = (bf16[256,128]{1,0:T(8,128)(2,1)S(1)}, bf16[256,128]{1,0:T(8,128)(2,1)}, u32[]{:S(2)}) copy-start(bf16[256,128]{1,0:T(8,128)(2,1)} %k_hbm.1) | copy-start | bytes 196612
  4.6 0.8 %copy-start.4 = (bf16[256,128]{1,0:T(8,128)(2,1)S(1)}, bf16[256,128]{1,0:T(8,128)(2,1)}, u32[]{:S(2)}) copy-start(bf16[256,128]{1,0:T(8,128)(2,1)} %v_hbm.1) | copy-start | bytes 196612
  5.4 0.7 %copy-start.5 = (f32[8,256]{1,0:T(8,128)S(1)}, f32[8,256]{1,0:T(8,128)}, u32[]{:S(2)}) copy-start(f32[8,256]{1,0:T(8,128)} %norm_hbm.1) | copy-start | bytes 24580
  6.1 0.7 %copy-start.6 = (s32[512]{0:T(512)S(1)}, s32[512]{0:T(512)}, u32[]{:S(2)}) copy-start(s32[512]{0:T(512)} %pos_ref.1) | copy-start | bytes 6148
where the time goes:
time: 55.5 us; the launch traced here: 55.1 us
  Pallas kernels  46.3 us (83%)
  local copies, waits for them, and re-layouts  8.23 us (15%)
  between operations  0.66 us (1%)
    pallas_call x1, Pallas kernels, local(): pl.pallas_call(functools.partial(kernel, sizes), out_shape=(jax.ShapeDtyp...  46.3 us
    unnamed x17, local copies, waits for them, and re-layouts  8.23 us

commit v1 on v0

--- a/solution.py
+++ b/solution.py
@@ -15,19 +15,47 @@
 
 FAR = -1
 STEPS = (
-    (0, 0, 0),
     (1, 0, 0),
     (1, 0, 1),
+    (2, 0, 1),
+    (1, 1, 1),
+    (1, 1, 0),
+    (FAR, 1, 1),
+    (2, 1, 1),
+    (2, 1, 0),
+    (FAR, 0, 1),
     (0, 1, 0),
-    (1, 1, 0),
-    (1, 1, 1),
     (2, 0, 0),
-    (2, 0, 1),
-    (2, 1, 0),
-    (2, 1, 1),
-    (FAR, 1, 1),
-    (FAR, 0, 1),
+    (0, 0, 0),
 )
+EVENTS = {
+    0: (("in 10", "in 01"),),
+    1: (("swap",),),
+    2: (("in 20", "out 10"),),
+    3: (("in 11",),),
+    5: (("out 11",), ("in 31", "out 11")),
+    6: (("in 21",), ("in 21", "out 31")),
+    8: (("out 21",), ("in 30", "out 21")),
+    9: ((), ("out 30",)),
+    10: (("out 01",),),
+    11: (("out 20",),),
+}
+FORWARD = {
+    "11": ("10", 0, 1),
+    "20": ("10", 1, 0),
+    "21": ("20", 0, 1),
+    "30": ("20", 1, 0),
+    "31": ("01", 3, 0),
+}
+RETURN = {
+    "01": "home",
+    "10": "home",
+    "11": "z",
+    "20": "home",
+    "21": "x",
+    "30": "z",
+    "31": "x",
+}
 
 
 def dot(a, b):
@@ -44,18 +72,20 @@
 
 def kernel(
     sizes,
-    q_hbm, k_hbm, v_hbm, o_hbm, g_hbm, norm_hbm, pos_ref,
+    q_hbm, k_hbm, v_hbm, o_hbm, g_hbm, norm_hbm, pos_hbm,
     dq_out, dk_out, dv_out,
     qs, gs, os, qt, gt, kv, norm, cols, cols_in, lse, delta, hidden,
-    dq, dkv, staged, from_x, from_z, dq_send, dq_recv, dq_final, dkv_final,
-    load_q, load_g, load_o, load_kv, load_norm, store_dq, store_dkv,
-    swap_send, swap_recv, fwd_send, fwd_recv, ret_send, x_recv, z_recv,
+    dq, dkv, staged, merged, home, dq_send, dq_recv, dq_final, dkv_final, pos_ref,
+    load_q, load_g, load_o, load_kv, load_norm, load_pos, store_dq, store_dkv,
+    swap_send, swap_recv, fwd_send, fwd_recv, ret_send, merge_recv, home_recv,
 ):
     n_outer, n_inner, heads, rows, hd = sizes
     shard = rows // 2
     scale = hd**-0.5
     outer, inner = lax.axis_index("outer"), lax.axis_index("inner")
     core = lax.rem(outer, 2)
+    on_core0 = pl.when(core == 0)
+    on_core1 = pl.when(core == 1)
 
     def chip(dc, e=0):
         return (
@@ -83,6 +113,7 @@
         pltpu.make_async_copy(ref, kv.at[0, n], load_kv.at[n])
         for n, ref in enumerate((k_hbm, v_hbm))
     ]
+    pos_load = pltpu.make_async_copy(pos_hbm, pos_ref, load_pos)
     norm_load = pltpu.make_async_copy(norm_hbm, norm, load_norm)
     q_loads = loads(q_hbm, qs.at[0], load_q)
     g_loads = loads(g_hbm, gs.at[0], load_g)
@@ -93,45 +124,56 @@
     swap_cols = remote(cols, cols_in, swap_send.at[2], swap_recv.at[2], sibling)
     swap_dq = remote(dq_send, dq_recv, swap_send.at[3], swap_recv.at[3], sibling)
 
-    def to_z(dc):
-        return remote(
-            kv.at[2 * dc], kv.at[2 * dc + 2], fwd_send.at[2 * dc], fwd_recv.at[2 * dc + 2], chip(1)
-        )
-
-    def to_x(dc):
-        return remote(
-            kv.at[2 * dc], kv.at[2 * dc + 1], fwd_send.at[2 * dc + 1], fwd_recv.at[2 * dc + 1],
-            chip(0, 1),
-        )
-
-    def back_x(dc):
-        slot = 2 * dc + 1
-        return remote(
-            staged.at[slot], from_x.at[dc], ret_send.at[slot], x_recv.at[dc], chip(0, -1)
-        )
-
-    def back_z(dc):
-        slot = 2 * dc
-        return remote(
-            staged.at[slot], from_z.at[dc], ret_send.at[slot], z_recv.at[dc], chip(-dc)
-        )
-
-    for copy in (*kv_loads, *q_loads, *g_loads, norm_load, *o_loads):
+    def slot_of(name):
+        return 2 * int(name[0]) + int(name[1])
+
+    def on_core(name):
+        return on_core1 if name[0] == "3" else lambda body: body()
+
+    sources = {"10": ("own", 1, 0), "01": ("own", 0, 1), **FORWARD}
+
+    def forward(name):
+        source, dc, e = sources[name]
+        src, dst = 0 if source == "own" else slot_of(source), slot_of(name)
+        return remote(kv.at[src], kv.at[dst], fwd_send.at[dst], fwd_recv.at[dst], chip(dc, e))
+
+    def send_on(source):
+        for name, (before, _, _) in sources.items():
+            if before == source:
+                on_core(name)(lambda name=name: forward(name).start())
+
+    def arrival(ref, sem, slot):
+        return remote(ref.at[slot], ref.at[slot], fwd_send.at[slot], sem.at[slot], sibling)
+
+    def onto(name):
+        return {"home": "00", "x": name[0] + "0", "z": str(int(name[0]) - 1) + name[1]}[RETURN[name]]
+
+    def back(name):
+        slot = slot_of(name)
+        if RETURN[name] == "home":
+            ref, sem, to = home, home_recv, chip(-int(name[0]), -int(name[1]))
+        else:
+            ref, sem, to = merged, merge_recv, chip(-1) if RETURN[name] == "z" else chip(0, -1)
+        return remote(staged.at[slot], ref.at[slot], ret_send.at[slot], sem.at[slot], to)
+
+    for copy in (*kv_loads, *q_loads, *g_loads, norm_load, pos_load, *o_loads):
         copy.start()
-    partners = [sibling, chip(0, 1), chip(0, -1)]
-    for dc in (1, 2, 3):
-        partners += [chip(dc), chip(-dc)]
     barrier = pltpu.get_barrier_semaphore()
-    for partner in partners:
-        pl.semaphore_signal(barrier, inc=1, device_id=partner, device_id_type=MESH)
+
+    def greet(device):
+        pl.semaphore_signal(barrier, inc=1, device_id=device, device_id_type=MESH)
+
+    greet(sibling)
+    reached = sorted({(dc, e) for _, dc, e in sources.values()})
+    for dc, e in reached:
+        greet(chip(-dc, -e))
 
     dkv[...] = jnp.zeros_like(dkv)
     dq[...] = jnp.zeros_like(dq)
     for copy in kv_loads:
         copy.wait()
-    pl.semaphore_wait(barrier, len(partners))
-    to_z(0).start()
-    to_x(0).start()
+    pl.semaphore_wait(barrier, 1 + len(reached))
+    send_on("own")
     for copy in q_loads:
         copy.wait()
     swap_q.start()
@@ -140,6 +182,7 @@
     swap_g.start()
 
     norm_load.wait()
+    pos_load.wait()
     lane = lax.broadcasted_iota(jnp.int32, (rows, hd), 1)
     padded = jnp.concatenate([norm[...] * LOG2E, jnp.zeros((hd - heads, rows), F32)], 0)
     cols[0] = padded.T
@@ -209,86 +252,56 @@
 
     far = 3 * core
 
-    def on_far(body):
-        pl.when(core == 1)(body)
-
-    def send_x(dc):
-        staged[2 * dc + 1] = dkv[2 * dc + 1].astype(BF16)
-        back_x(dc).start()
-
-    def send_z(dc):
-        back_x(dc).wait_recv()
-        staged[2 * dc] = (dkv[2 * dc] + from_x[dc].astype(F32)).astype(BF16)
-        back_z(dc).start()
-
-    def before(t):
-        @pl.when(t == 1)
-        def _():
-            to_z(0).wait_recv()
-            to_z(1).start()
-            to_x(1).start()
+    def act(what):
+        if what == "swap":
             swap_q.wait_recv()
             swap_g.wait_recv()
             swap_cols.wait_recv()
             prepare(1, cols_in)
-
-        @pl.when(t == 3)
-        def _():
-            to_x(0).wait_recv()
-
-        @pl.when(t == 4)
-        def _():
-            to_z(1).wait_recv()
-            on_far(lambda: to_z(2).start())
-            to_x(2).start()
-            to_x(1).wait_recv()
-
-        @pl.when((t == 7) & (core == 1))
-        def _():
-            to_z(2).wait_recv()
-            to_x(3).start()
-
-        @pl.when(t == 8)
-        def _():
-            to_x(2).wait_recv()
-
-        @pl.when((t == 10) & (core == 1))
-        def _():
-            to_x(3).wait_recv()
-
-    def after(t):
-        @pl.when(t == 5)
-        def _():
-            send_x(1)
-
-        @pl.when(t == 7)
-        def _():
-            send_z(1)
-
-        @pl.when(t == 9)
-        def _():
-            send_x(2)
-
-        @pl.when(t == 10)
-        def _():
-            send_x(0)
-            on_far(lambda: send_x(3))
+            return
+        kind, name = what.split()
+        slot = slot_of(name)
+        if kind == "in":
+            arrival(kv, fwd_recv, slot).wait_recv()
+            send_on(name)
+            return
+        for other in [other for other in RETURN if onto(other) == name]:
+
+            @on_core(other)
+            def _(other=slot_of(other)):
+                arrival(merged, merge_recv, other).wait_recv()
+                dkv[slot] += merged[other].astype(F32)
+
+        staged[slot] = dkv[slot].astype(BF16)
+        back(name).start()
+
+    def events_at(n, here):
+        if n not in EVENTS:
+            return
+        by_core = EVENTS[n]
+        if len(by_core) == 1:
+            pl.when(here)(lambda: [act(what) for what in by_core[0]] and None)
+            return
+        for index, events in enumerate(by_core):
+            if events:
+                pl.when(here & (core == index))(
+                    lambda events=events: [act(what) for what in events] and None
+                )
 
     def body(t, carry):
-        before(t)
+        for n in range(len(STEPS)):
+            events_at(n, t == n)
         dc = at_step(t, [far if dc == FAR else dc for dc, _, _ in STEPS])
         e = at_step(t, [e for _, e, _ in STEPS])
         side = at_step(t, [side for _, _, side in STEPS])
         step(side, dc, e)
-        after(t)
         return carry
 
     lax.fori_loop(0, len(STEPS), body, 0)
 
     dq_send[...] = dq[1].astype(BF16)
     swap_dq.start()
-    send_z(2)
-    on_far(lambda: send_z(3))
+    events_at(len(STEPS), core >= 0)
 
     swap_dq.wait_recv()
     stores = []
@@ -301,16 +314,13 @@
         copy.start()
         stores.append(copy)
 
-    back_x(0).wait_recv()
-    back_z(1).wait_recv()
-    dkv[0] += from_x[0].astype(F32) + from_z[1].astype(F32)
-    back_z(2).wait_recv()
-    dkv[0] += from_z[2].astype(F32)
-
-    @pl.when(core == 1)
-    def _():
-        back_z(3).wait_recv()
-        dkv[0] += from_z[3].astype(F32)
+    for name in RETURN:
+        if RETURN[name] == "home":
+
+            @on_core(name)
+            def _(slot=slot_of(name)):
+                arrival(home, home_recv, slot).wait_recv()
+                dkv[0] += home[slot].astype(F32)
 
     dkv_final[0] = dkv[0, 0].T.astype(BF16)
     dkv_final[1] = dkv[0, 1].T.astype(BF16)
@@ -321,17 +331,27 @@
 
     for copy in (swap_q, swap_g, swap_cols, swap_dq):
         copy.wait_send()
-    for copy in (to_z(0), to_z(1), to_x(0), to_x(1), to_x(2)):
-        copy.wait_send()
-    for copy in (back_x(0), back_x(1), back_x(2), back_z(1), back_z(2)):
-        copy.wait_send()
-
-    @pl.when(core == 1)
-    def _():
-        for copy in (to_z(2), to_x(3), back_x(3), back_z(3)):
-            copy.wait_send()
+    for name in sources:
+
+        @on_core(name)
+        def _(name=name):
+            forward(name).wait_send()
+            back(name).wait_send()
 
     for copy in stores:
+        copy.wait()
+
+
+def store(*refs):
+    bufs, sems = refs[6:9], refs[9]
+    into = [pltpu.make_async_copy(refs[n], bufs[n], sems.at[n]) for n in range(3)]
+    out = [pltpu.make_async_copy(bufs[n], refs[3 + n], sems.at[3 + n]) for n in range(3)]
+    for copy in into:
+        copy.start()
+    for n in range(3):
+        into[n].wait()
+        out[n].start()
+    for copy in out:
         copy.wait()
 
 
@@ -357,16 +377,18 @@
         pltpu.VMEM((2, flat, hd), F32),
         pltpu.VMEM((8, 2, hd, rows), F32),
         pltpu.VMEM((8, 2, hd, rows), BF16),
-        pltpu.VMEM((4, 2, hd, rows), BF16),
-        pltpu.VMEM((4, 2, hd, rows), BF16),
+        pltpu.VMEM((8, 2, hd, rows), BF16),
+        pltpu.VMEM((8, 2, hd, rows), BF16),
         pltpu.VMEM((flat, hd), BF16),
         pltpu.VMEM((flat, hd), BF16),
         pltpu.VMEM((flat, hd), BF16),
         pltpu.VMEM((2, rows, hd), BF16),
+        pltpu.SMEM(shard_pos.shape, jnp.int32),
         dma((heads,)),
         dma((heads,)),
         dma((heads,)),
         dma((2,)),
+        dma,
         dma,
         dma((heads,)),
         dma((2,)),
@@ -375,25 +397,33 @@
         dma((8,)),
         dma((8,)),
         dma((8,)),
-        dma((4,)),
-        dma((4,)),
+        dma((8,)),
+        dma((8,)),
     ]
-    hbm = pl.BlockSpec(memory_space=pl.ANY)
-    return pl.pallas_call(
+    hbm = pl.BlockSpec(memory_space=pltpu.HBM)
+    grads = pl.pallas_call(
         functools.partial(kernel, sizes),
         out_shape=(
             jax.ShapeDtypeStruct(queries.shape, BF16),
             jax.ShapeDtypeStruct(key_rows.shape, BF16),
             jax.ShapeDtypeStruct(value_rows.shape, BF16),
         ),
-        in_specs=[hbm] * 6 + [pl.BlockSpec(memory_space=pltpu.SMEM)],
+        in_specs=[hbm] * 7,
         out_specs=(hbm,) * 3,
         scratch_shapes=scratch,
         compiler_params=pltpu.CompilerParams(
-            collective_id=0, has_side_effects=True, vmem_limit_bytes=48 * 2**20
+            collective_id=0, has_side_effects=True, vmem_limit_bytes=63 * 2**20
         ),
         name="window_grads",
     )(queries, key_rows, value_rows, outputs, out_grad, log_norm, shard_pos)
+    return pl.pallas_call(
+        store,
+        out_shape=[jax.ShapeDtypeStruct(grad.shape, grad.dtype) for grad in grads],
+        in_specs=[hbm] * 3,
+        out_specs=[hbm] * 3,
+        scratch_shapes=[pltpu.VMEM(grad.shape, grad.dtype) for grad in grads] + [dma((6,))],
+        name="store",
+    )(*grads)
 
 
 def solution(mesh):

time: 55.5 us -> 45.5 us (0.82)
  local copies, waits for them, and re-layouts: 8.23 us -> 0 us
  Pallas kernels: 46.3 us -> 44.7 us
    unnamed x17 -> x0, local copies, waits for them, and re-layouts: 8.23 us -> none
    pallas_call x1, Pallas kernels: 46.3 us -> 42.8 us  [local(): pl.pallas_call(functools.partial(kernel, sizes), out_shape=(jax.ShapeDtyp...]
    pallas_call x0 -> x1, Pallas kernels: none -> 1.92 us  [local(): pl.pallas_call(store, out_shape=[jax.ShapeDtypeStruct(grad.shape, grad.dt...]
where the time goes in v1:
time: 45.5 us; the launch traced here: 45.3 us
  Pallas kernels  44.7 us (98%)
  between operations  0.64 us (1%)
    pallas_call x1, Pallas kernels, local(): pl.pallas_call(functools.partial(kernel, sizes), out_shape=(jax.ShapeDtyp...  42.8 us
    pallas_call x1, Pallas kernels, local(): pl.pallas_call(store, out_shape=[jax.ShapeDtypeStruct(grad.shape, grad.dt...  1.92 us

profile of v1, /device:TPU:7, one launch (start us, length us, event | category | flops | bytes accessed | tf_op | source)
XLA Modules:
  0.0 45.3 jit_solution(9789582530183179141)
XLA Ops:
  0.6 42.8 %window_grads.1 = (bf16[256,1024]{1,0:T(8,128)(2,1)}, bf16[256,128]{1,0:T(8,128)(2,1)}, bf16[256,128]{1,0:T(8,128)(2,1)}) custom-call(bf16[256,1024]{1,0:T(8,128)(2,1)} %q_hbm.1, bf16[256,128]{1,0:T(8,128)(2,1)} %k_hbm.1, bf16[256,128]{1,0:T(8,128)(2,1)} %v_hbm.1, bf16[256,1024]{1,0:T(8,128)(2,1)} %o_hbm.1, bf16[256,1024]{1,0:T(8,128)(2,1)} %g_hbm.1, ...), custom_call_target="tpu_custom_call" | custom-call | tf_op jit(solution)/shard_map/window_grads/pallas_call | solution.py:404
  43.4 1.9 %store.1 = (bf16[256,1024]{1,0:T(8,128)(2,1)}, bf16[256,128]{1,0:T(8,128)(2,1)}, bf16[256,128]{1,0:T(8,128)(2,1)}) custom-call(bf16[256,1024]{1,0:T(8,128)(2,1)} %get-tuple-element.6.refs_0_, bf16[256,128]{1,0:T(8,128)(2,1)} %get-tuple-element.7.refs_1_, bf16[256,128]{1,0:T(8,128)(2,1)} %get-tuple-element.8.refs_2_), custom_call_target="tpu_custom_call" | custom-call | tf_op jit(solution)/shard_map/store/pallas_call | solution.py:419

commit v2 on v1

--- a/solution.py
+++ b/solution.py
@@ -15,45 +15,46 @@
 
 FAR = -1
 STEPS = (
-    (1, 0, 0),
     (1, 0, 1),
+    (2, 0, 0),
     (2, 0, 1),
     (1, 1, 1),
     (1, 1, 0),
+    (2, 1, 0),
+    (2, 1, 1),
+    (1, 0, 0),
+    (0, 1, 0),
     (FAR, 1, 1),
-    (2, 1, 1),
-    (2, 1, 0),
+    (0, 0, 0),
     (FAR, 0, 1),
-    (0, 1, 0),
-    (2, 0, 0),
-    (0, 0, 0),
 )
 EVENTS = {
-    0: (("in 10", "in 01"),),
-    1: (("swap",),),
-    2: (("in 20", "out 10"),),
-    3: (("in 11",),),
-    5: (("out 11",), ("in 31", "out 11")),
-    6: (("in 21",), ("in 21", "out 31")),
-    8: (("out 21",), ("in 30", "out 21")),
-    9: ((), ("out 30",)),
-    10: (("out 01",),),
-    11: (("out 20",),),
+    0: (("in 10", "swap"),),
+    1: (("in 20",),),
+    3: (("in 11", "out 20"),),
+    5: (("in 21", "out 11"),),
+    6: (("in 01",),),
+    7: (("out 21",),),
+    8: (("out 10",), ("out 10", "in 31")),
+    9: ((), ("out 01",)),
+    10: (("out 01",), ("out 31",)),
+    11: ((), ("in 30",)),
+    12: ((), ("out 30",)),
 }
 FORWARD = {
     "11": ("10", 0, 1),
     "20": ("10", 1, 0),
     "21": ("20", 0, 1),
     "30": ("20", 1, 0),
-    "31": ("01", 3, 0),
+    "31": ("21", 1, 0),
 }
 RETURN = {
     "01": "home",
     "10": "home",
-    "11": "z",
-    "20": "home",
-    "21": "x",
-    "30": "z",
+    "11": "x",
+    "20": "z",
+    "21": "home",
+    "30": "home",
     "31": "x",
 }
 
@@ -75,8 +76,8 @@
     q_hbm, k_hbm, v_hbm, o_hbm, g_hbm, norm_hbm, pos_hbm,
     dq_out, dk_out, dv_out,
     qs, gs, os, qt, gt, kv, norm, cols, cols_in, lse, delta, hidden,
-    dq, dkv, staged, merged, home, dq_send, dq_recv, dq_final, dkv_final, pos_ref,
-    load_q, load_g, load_o, load_kv, load_norm, load_pos, store_dq, store_dkv,
+    dq, dkv, staged, merged, home, dq_send, dq_recv, pos_ref,
+    load_q, load_g, load_o, load_kv, load_norm, load_pos,
     swap_send, swap_recv, fwd_send, fwd_recv, ret_send, merge_recv, home_recv,
 ):
     n_outer, n_inner, heads, rows, hd = sizes
@@ -304,15 +305,10 @@
     events_at(len(STEPS), core >= 0)
 
     swap_dq.wait_recv()
-    stores = []
     for h in range(heads):
         part = pl.ds(h * rows, rows)
-        dq_final[part, :] = (dq[0, part, :] + dq_recv[part, :].astype(F32)).astype(BF16)
-        copy = pltpu.make_async_copy(
-            dq_final.at[part], dq_out.at[:, pl.ds(h * hd, hd)], store_dq.at[h]
-        )
-        copy.start()
-        stores.append(copy)
+        total = dq[0, part, :] + dq_recv[part, :].astype(F32)
+        dq_out[:, h * hd : (h + 1) * hd] = total.astype(BF16)
 
     for name in RETURN:
         if RETURN[name] == "home":
@@ -322,12 +318,8 @@
                 arrival(home, home_recv, slot).wait_recv()
                 dkv[0] += home[slot].astype(F32)
 
-    dkv_final[0] = dkv[0, 0].T.astype(BF16)
-    dkv_final[1] = dkv[0, 1].T.astype(BF16)
-    for n, ref in enumerate((dk_out, dv_out)):
-        copy = pltpu.make_async_copy(dkv_final.at[n], ref, store_dkv.at[n])
-        copy.start()
-        stores.append(copy)
+    dk_out[...] = dkv[0, 0].T.astype(BF16)
+    dv_out[...] = dkv[0, 1].T.astype(BF16)
 
     for copy in (swap_q, swap_g, swap_cols, swap_dq):
         copy.wait_send()
@@ -338,20 +330,14 @@
             forward(name).wait_send()
             back(name).wait_send()
 
-    for copy in stores:
-        copy.wait()
-
 
 def store(*refs):
-    bufs, sems = refs[6:9], refs[9]
-    into = [pltpu.make_async_copy(refs[n], bufs[n], sems.at[n]) for n in range(3)]
-    out = [pltpu.make_async_copy(bufs[n], refs[3 + n], sems.at[3 + n]) for n in range(3)]
-    for copy in into:
+    copies = [
+        pltpu.make_async_copy(refs[n], refs[3 + n], refs[6].at[n]) for n in range(3)
+    ]
+    for copy in copies:
         copy.start()
-    for n in range(3):
-        into[n].wait()
-        out[n].start()
-    for copy in out:
+    for copy in copies:
         copy.wait()
 
 
@@ -381,8 +367,6 @@
         pltpu.VMEM((8, 2, hd, rows), BF16),
         pltpu.VMEM((flat, hd), BF16),
         pltpu.VMEM((flat, hd), BF16),
-        pltpu.VMEM((flat, hd), BF16),
-        pltpu.VMEM((2, rows, hd), BF16),
         pltpu.SMEM(shard_pos.shape, jnp.int32),
         dma((heads,)),
         dma((heads,)),
@@ -390,8 +374,6 @@
         dma((2,)),
         dma,
         dma,
-        dma((heads,)),
-        dma((2,)),
         dma((4,)),
         dma((4,)),
         dma((8,)),
@@ -401,29 +383,30 @@
         dma((8,)),
     ]
     hbm = pl.BlockSpec(memory_space=pltpu.HBM)
+    vmem = pl.BlockSpec(memory_space=pltpu.VMEM)
     grads = pl.pallas_call(
         functools.partial(kernel, sizes),
         out_shape=(
-            jax.ShapeDtypeStruct(queries.shape, BF16),
-            jax.ShapeDtypeStruct(key_rows.shape, BF16),
-            jax.ShapeDtypeStruct(value_rows.shape, BF16),
+            pltpu.VMEM(queries.shape, BF16),
+            pltpu.VMEM(key_rows.shape, BF16),
+            pltpu.VMEM(value_rows.shape, BF16),
         ),
         in_specs=[hbm] * 7,
-        out_specs=(hbm,) * 3,
+        out_specs=(vmem,) * 3,
         scratch_shapes=scratch,
         compiler_params=pltpu.CompilerParams(
-            collective_id=0, has_side_effects=True, vmem_limit_bytes=63 * 2**20
+            collective_id=0, has_side_effects=True, vmem_limit_bytes=56 * 2**20
         ),
         name="window_grads",
     )(queries, key_rows, value_rows, outputs, out_grad, log_norm, shard_pos)
     return pl.pallas_call(
         store,
         out_shape=[jax.ShapeDtypeStruct(grad.shape, grad.dtype) for grad in grads],
-        in_specs=[hbm] * 3,
+        in_specs=[vmem] * 3,
         out_specs=[hbm] * 3,
-        scratch_shapes=[pltpu.VMEM(grad.shape, grad.dtype) for grad in grads] + [dma((6,))],
+        scratch_shapes=[dma((3,))],
         name="store",
-    )(*grads)
+    )(*(pltpu.with_memory_space_constraint(grad, pltpu.VMEM) for grad in grads))
 
 
 def solution(mesh):

time: 45.5 us -> 43.4 us (0.954)
  Pallas kernels: 44.7 us -> 42.6 us
    pallas_call x1, Pallas kernels: 1.92 us -> 0.85 us  [local(): pl.pallas_call(store, out_shape=[jax.ShapeDtypeStruct(grad.shape, grad.dt...]
    pallas_call x1, Pallas kernels: 42.8 us -> 41.7 us  [local(): pl.pallas_call(functools.partial(kernel, sizes), out_shape=(pltpu.VMEM(qu...]
where the time goes in v2:
time: 43.4 us; the launch traced here: 43.2 us
  Pallas kernels  42.6 us (98%)
  between operations  0.64 us (1%)
    pallas_call x1, Pallas kernels, local(): pl.pallas_call(functools.partial(kernel, sizes), out_shape=(pltpu.VMEM(qu...  41.7 us

profile of v2, /device:TPU:7, one launch (start us, length us, event | category | flops | bytes accessed | tf_op | source)
XLA Modules:
  0.0 43.2 jit_solution(5354553214087469114)
XLA Ops:
  0.6 41.7 %window_grads.1 = (bf16[256,1024]{1,0:T(8,128)(2,1)S(1)}, bf16[256,128]{1,0:T(8,128)(2,1)S(1)}, bf16[256,128]{1,0:T(8,128)(2,1)S(1)}) custom-call(bf16[256,1024]{1,0:T(8,128)(2,1)} %q_hbm.1, bf16[256,128]{1,0:T(8,128)(2,1)} %k_hbm.1, bf16[256,128]{1,0:T(8,128)(2,1)} %v_hbm.1, bf16[256,1024]{1,0:T(8,128)(2,1)} %o_hbm.1, bf16[256,1024]{1,0:T(8,128)(2,1)} %g_hbm.1, ...), custom_call_target="tpu_custom_call" | custom-call | tf_op jit(solution)/shard_map/window_grads/pallas_call | solution.py:387
  42.4 0.9 %store.1 = (bf16[256,1024]{1,0:T(8,128)(2,1)}, bf16[256,128]{1,0:T(8,128)(2,1)}, bf16[256,128]{1,0:T(8,128)(2,1)}) custom-call(bf16[256,1024]{1,0:T(8,128)(2,1)S(1)} %get-tuple-element.6.refs_0_, bf16[256,128]{1,0:T(8,128)(2,1)S(1)} %get-tuple-element.7.refs_1_, bf16[256,128]{1,0:T(8,128)(2,1)S(1)} %get-tuple-element.8.refs_2_), custom_call_target="tpu_custom_call" | custom-call | tf_op jit(solution)/shard_map/store/pallas_call | solution.py:402

commit v3 on v2

--- a/solution.py
+++ b/solution.py
@@ -15,30 +15,27 @@
 
 FAR = -1
 STEPS = (
+    (0, 0, 0),
     (1, 0, 1),
     (2, 0, 0),
     (2, 0, 1),
+    (1, 1, 0),
     (1, 1, 1),
-    (1, 1, 0),
     (2, 1, 0),
     (2, 1, 1),
+    (0, 1, 0),
     (1, 0, 0),
-    (0, 1, 0),
     (FAR, 1, 1),
-    (0, 0, 0),
     (FAR, 0, 1),
 )
 EVENTS = {
-    0: (("in 10", "swap"),),
-    1: (("in 20",),),
-    3: (("in 11", "out 20"),),
-    5: (("in 21", "out 11"),),
-    6: (("in 01",),),
-    7: (("out 21",),),
-    8: (("out 10",), ("out 10", "in 31")),
-    9: ((), ("out 01",)),
-    10: (("out 01",), ("out 31",)),
-    11: ((), ("in 30",)),
+    1: (("in 10", "swap"),),
+    2: (("in 20",),),
+    4: (("in 11", "out 20"),),
+    6: (("in 21", "out 11"),),
+    8: (("in 01", "out 21"),),
+    10: (("out 10",), ("in 31", "out 10", "out 01")),
+    11: (("out 01",), ("in 30", "out 31")),
     12: ((), ("out 30",)),
 }
 FORWARD = {
@@ -143,6 +140,15 @@
             if before == source:
                 on_core(name)(lambda name=name: forward(name).start())
 
+    def send_own():
+        for name, (before, dc, e) in sources.items():
+            if before == "own":
+                dst = slot_of(name)
+                for n, ref in enumerate((k_hbm, v_hbm)):
+                    remote(
+                        ref, kv.at[dst, n], fwd_send.at[dst], fwd_recv.at[dst], chip(dc, e)
+                    ).start()
+
     def arrival(ref, sem, slot):
         return remote(ref.at[slot], ref.at[slot], fwd_send.at[slot], sem.at[slot], sibling)
 
@@ -157,30 +163,31 @@
             ref, sem, to = merged, merge_recv, chip(-1) if RETURN[name] == "z" else chip(0, -1)
         return remote(staged.at[slot], ref.at[slot], ret_send.at[slot], sem.at[slot], to)
 
-    for copy in (*kv_loads, *q_loads, *g_loads, norm_load, pos_load, *o_loads):
-        copy.start()
     barrier = pltpu.get_barrier_semaphore()
 
     def greet(device):
         pl.semaphore_signal(barrier, inc=1, device_id=device, device_id_type=MESH)
 
-    greet(sibling)
     reached = sorted({(dc, e) for _, dc, e in sources.values()})
     for dc, e in reached:
         greet(chip(-dc, -e))
-
-    dkv[...] = jnp.zeros_like(dkv)
-    dq[...] = jnp.zeros_like(dq)
+    greet(sibling)
+    for copy in (*kv_loads, *q_loads, *g_loads):
+        copy.start()
+    pl.semaphore_wait(barrier, 1 + len(reached))
+    send_own()
     for copy in kv_loads:
         copy.wait()
-    pl.semaphore_wait(barrier, 1 + len(reached))
-    send_on("own")
+    for copy in (*o_loads, norm_load, pos_load):
+        copy.start()
     for copy in q_loads:
         copy.wait()
     swap_q.start()
     for copy in g_loads:
         copy.wait()
     swap_g.start()
+    dkv[...] = jnp.zeros_like(dkv)
+    dq[...] = jnp.zeros_like(dq)
 
     norm_load.wait()
     pos_load.wait()

time: 43.4 us -> 42.4 us (0.977)
  Pallas kernels: 42.6 us -> 41.5 us
    pallas_call x1, Pallas kernels: 41.7 us -> 40.7 us  [local(): pl.pallas_call(functools.partial(kernel, sizes), out_shape=(pltpu.VMEM(qu...]
where the time goes in v3:
time: 42.4 us; the launch traced here: 42.2 us
  Pallas kernels  41.5 us (98%)
  between operations  0.64 us (2%)
    pallas_call x1, Pallas kernels, local(): pl.pallas_call(functools.partial(kernel, sizes), out_shape=(pltpu.VMEM(qu...  40.7 us
    pallas_call x1, Pallas kernels, local(): pl.pallas_call(store, out_shape=[jax.ShapeDtypeStruct(grad.shape, grad.dt...  0.85 us

profile of v3, /device:TPU:7, one launch (start us, length us, event | category | flops | bytes accessed | tf_op | source)
XLA Modules:
  0.0 42.2 jit_solution(12862993168933430247)
XLA Ops:
  0.6 40.7 %window_grads.1 = (bf16[256,1024]{1,0:T(8,128)(2,1)S(1)}, bf16[256,128]{1,0:T(8,128)(2,1)S(1)}, bf16[256,128]{1,0:T(8,128)(2,1)S(1)}) custom-call(bf16[256,1024]{1,0:T(8,128)(2,1)} %q_hbm.1, bf16[256,128]{1,0:T(8,128)(2,1)} %k_hbm.1, bf16[256,128]{1,0:T(8,128)(2,1)} %v_hbm.1, bf16[256,1024]{1,0:T(8,128)(2,1)} %o_hbm.1, bf16[256,1024]{1,0:T(8,128)(2,1)} %g_hbm.1, ...), custom_call_target="tpu_custom_call" | custom-call | tf_op jit(solution)/shard_map/window_grads/pallas_call | solution.py:394
  41.3 0.9 %store.1 = (bf16[256,1024]{1,0:T(8,128)(2,1)}, bf16[256,128]{1,0:T(8,128)(2,1)}, bf16[256,128]{1,0:T(8,128)(2,1)}) custom-call(bf16[256,1024]{1,0:T(8,128)(2,1)S(1)} %get-tuple-element.6.refs_0_, bf16[256,128]{1,0:T(8,128)(2,1)S(1)} %get-tuple-element.7.refs_1_, bf16[256,128]{1,0:T(8,128)(2,1)S(1)} %get-tuple-element.8.refs_2_), custom_call_target="tpu_custom_call" | custom-call | tf_op jit(solution)/shard_map/store/pallas_call | solution.py:409

commit v4 on v3

--- a/solution.py
+++ b/solution.py
@@ -273,14 +273,11 @@
             arrival(kv, fwd_recv, slot).wait_recv()
             send_on(name)
             return
+        total = dkv[slot]
         for other in [other for other in RETURN if onto(other) == name]:
-
-            @on_core(other)
-            def _(other=slot_of(other)):
-                arrival(merged, merge_recv, other).wait_recv()
-                dkv[slot] += merged[other].astype(F32)
-
-        staged[slot] = dkv[slot].astype(BF16)
+            arrival(merged, merge_recv, slot_of(other)).wait_recv()
+            total += merged[slot_of(other)].astype(F32)
+        staged[slot] = total.astype(BF16)
         back(name).start()
 
     def events_at(n, here):
@@ -307,9 +304,9 @@
 
     lax.fori_loop(0, len(STEPS), body, 0)
 
+    events_at(len(STEPS), core >= 0)
     dq_send[...] = dq[1].astype(BF16)
     swap_dq.start()
-    events_at(len(STEPS), core >= 0)
 
     swap_dq.wait_recv()
     for h in range(heads):
@@ -317,10 +314,16 @@
         total = dq[0, part, :] + dq_recv[part, :].astype(F32)
         dq_out[:, h * hd : (h + 1) * hd] = total.astype(BF16)
 
+    total = dkv[0]
     for name in RETURN:
-        if RETURN[name] == "home":
-
-            @on_core(name)
+        if RETURN[name] == "home" and name[0] != "3":
+            arrival(home, home_recv, slot_of(name)).wait_recv()
+            total += home[slot_of(name)].astype(F32)
+    dkv[0] = total
+    for name in RETURN:
+        if RETURN[name] == "home" and name[0] == "3":
+
+            @on_core1
             def _(slot=slot_of(name)):
                 arrival(home, home_recv, slot).wait_recv()
                 dkv[0] += home[slot].astype(F32)

time: 42.4 us -> 42.4 us (level)
  no operation moved by 1% of the time
where the time goes in v4:
time: 42.4 us; the launch traced here: 42.1 us
  Pallas kernels  41.5 us (98%)
  between operations  0.64 us (2%)
    pallas_call x1, Pallas kernels, local(): pl.pallas_call(functools.partial(kernel, sizes), out_shape=(pltpu.VMEM(qu...  40.6 us
    pallas_call x1, Pallas kernels, local(): pl.pallas_call(store, out_shape=[jax.ShapeDtypeStruct(grad.shape, grad.dt...  0.85 us

profile of v4, /device:TPU:7, one launch (start us, length us, event | category | flops | bytes accessed | tf_op | source)
XLA Modules:
  0.0 42.1 jit_solution(7684558773698832878)
XLA Ops:
  0.6 40.6 %window_grads.1 = (bf16[256,1024]{1,0:T(8,128)(2,1)S(1)}, bf16[256,128]{1,0:T(8,128)(2,1)S(1)}, bf16[256,128]{1,0:T(8,128)(2,1)S(1)}) custom-call(bf16[256,1024]{1,0:T(8,128)(2,1)} %q_hbm.1, bf16[256,128]{1,0:T(8,128)(2,1)} %k_hbm.1, bf16[256,128]{1,0:T(8,128)(2,1)} %v_hbm.1, bf16[256,1024]{1,0:T(8,128)(2,1)} %o_hbm.1, bf16[256,1024]{1,0:T(8,128)(2,1)} %g_hbm.1, ...), custom_call_target="tpu_custom_call" | custom-call | tf_op jit(solution)/shard_map/window_grads/pallas_call | solution.py:397
  41.3 0.9 %store.1 = (bf16[256,1024]{1,0:T(8,128)(2,1)}, bf16[256,128]{1,0:T(8,128)(2,1)}, bf16[256,128]{1,0:T(8,128)(2,1)}) custom-call(bf16[256,1024]{1,0:T(8,128)(2,1)S(1)} %get-tuple-element.6.refs_0_, bf16[256,128]{1,0:T(8,128)(2,1)S(1)} %get-tuple-element.7.refs_1_, bf16[256,128]{1,0:T(8,128)(2,1)S(1)} %get-tuple-element.8.refs_2_), custom_call_target="tpu_custom_call" | custom-call | tf_op jit(solution)/shard_map/store/pallas_call | solution.py:412
